TPU v7x, 32 devices: a whole 2x2x4 slice. The times are simulated.
32 devices in a mesh: dp: 4 (over y, x), expert: 8 (over z, core).
Axes of the slice: x: 2, y: 2, z: 4, core: 2. Of those that a mesh axis runs over, the one named last changes fastest.
Arguments:
- output_grad: bfloat16 [6144, 2048], P(('dp', 'expert')), may hold values from -3 to 3
- routes: int32 [6144, 2], P(('dp', 'expert')), may hold values from 0 to 7, all different within a row; in each aligned block of 192 rows (0 to 191, 192 to 383, ...) at most 72 rows name the same one
- combine_weights: bfloat16 [6144, 2], P(('dp', 'expert')), may hold values from 0.049804688 to 0.5
- saved_hidden: bfloat16 [18432, 768], P(('dp', 'expert')), may hold values from -0.796875 to 0.796875
- down_weight: bfloat16 [8, 768, 2048], P('expert', 'dp'), may hold values from -0.21875 to 0.21875
Outputs:
- hidden_grad: bfloat16 [18432, 768], P(('dp', 'expert'))
- weight_grad: float32 [8, 768, 2048], P('expert', 'dp')
- route_grad: float32 [6144, 2], P(('dp', 'expert'))
Inputs may be any that keep to these rules, and one draw needn't show every extreme that they name: Each token names 2 different experts; among the 192 rows of one device no expert is named by more than 72 routes.
All inputs are finite; a program needn't handle non-finite values.
Results may differ from a plain program's by a relative error of at most 0.008.
Values may be sent and summed in bfloat16 or wider, within the bound.
A program may use at most 64 MiB of HBM per device.

v0:
```python
import jax
import jax.numpy as jnp
from jax import lax
from jax.sharding import PartitionSpec as P


def route_slots(routes, experts, capacity):
    flat_ids = routes.reshape(-1)
    place = jnp.arange(flat_ids.shape[0], dtype=jnp.int32)
    same = flat_ids[:, None] == flat_ids[None, :]
    rank = jnp.sum((same & (place[None, :] < place[:, None])).astype(jnp.int32), axis=1)
    return flat_ids * capacity + rank


def per_device(output_grad, routes, combine_weights, saved_hidden, down_weight):
    experts = lax.axis_size("expert")
    slot_count = saved_hidden.shape[0]
    capacity = slot_count // experts
    features = output_grad.shape[1]
    route_total = routes.shape[0] * routes.shape[1]
    target = route_slots(routes, experts, capacity)
    source = (
        jnp.full((slot_count,), route_total, jnp.int32)
        .at[target]
        .set(jnp.arange(route_total, dtype=jnp.int32))
    )
    is_live = source < route_total
    safe_index = jnp.where(is_live, source, 0)
    send_rows = jnp.where(
        is_live[:, None], output_grad[safe_index // routes.shape[1]], jnp.zeros((), jnp.bfloat16)
    )
    send_weights = jnp.where(
        is_live, combine_weights.reshape(-1)[safe_index], jnp.zeros((), jnp.bfloat16)
    )
    recv_rows, recv_weights = (
        lax.all_to_all(
            send_rows.reshape(experts, capacity, features),
            "expert",
            split_axis=0,
            concat_axis=0,
            tiled=True,
        ),
        lax.all_to_all(
            send_weights.reshape(experts, capacity),
            "expert",
            split_axis=0,
            concat_axis=0,
            tiled=True,
        ),
    )
    grad_rows = recv_rows.reshape(slot_count, features)
    slot_weights = recv_weights.reshape(slot_count).astype(jnp.float32)
    weighted = (slot_weights[:, None] * grad_rows.astype(jnp.float32)).astype(jnp.bfloat16)
    weight_shard = down_weight[0]
    contract = (((1,), (1,)), ((), ()))
    full_weight = lax.all_gather(weight_shard, "dp", axis=0, tiled=True)
    unscaled = lax.dot_general(grad_rows, full_weight, contract, preferred_element_type=jnp.float32)
    route_terms = jnp.sum(saved_hidden.astype(jnp.float32) * unscaled, axis=1)
    hidden_grad = (slot_weights[:, None] * unscaled).astype(jnp.bfloat16)
    grad_part = lax.psum_scatter(
        lax.dot_general(
            saved_hidden, weighted, (((0,), (0,)), ((), ())), preferred_element_type=jnp.float32
        ).astype(jnp.bfloat16),
        "dp",
        scatter_dimension=0,
        tiled=True,
    ).astype(jnp.float32)
    returned = lax.all_to_all(
        route_terms.reshape(experts, capacity), "expert", split_axis=0, concat_axis=0, tiled=True
    )
    route_grad = returned.reshape(-1)[target].reshape(routes.shape)
    return (hidden_grad, grad_part[None], route_grad)


def solution(mesh):
    return jax.shard_map(
        per_device,
        mesh=mesh,
        in_specs=(
            P(("dp", "expert"), None),
            P(("dp", "expert"), None),
            P(("dp", "expert"), None),
            P(("dp", "expert"), None),
            P("expert", "dp", None),
        ),
        out_specs=(P(("dp", "expert"), None), P("expert", "dp", None), P(("dp", "expert"), None)),
        check_vma=False,
    )
```

profile of v0, /device:TPU:0, one launch (start us, length us, event | category | flops | bytes accessed | tf_op | source)
XLA Modules:
  0.0 155.5 jit_solution(9721528789717610883)
XLA Ops:
  7.2 0.9 copy.21
  8.1 0.7 broadcast_multiply_fusion
  8.7 0.1 eq.15
  8.9 0.2 convert_reduce_fusion
  9.1 0.1 copy.20
  9.2 0.1 mul.37
  9.4 2.9 %scatter_custom_fusion = s32[576]{0:T(1024)S(1)} fusion(s32[384]{0:T(512)S(1)} %fusion.9, s32[384]{0:T(512)S(1)} %iota.10, s32[]{:T(128)} %constant.9.clone.1), kind=kCustom, calls=%fused_computation.32 | custom fusion | bytes 2308 | tf_op jit(solution)/shard_map/scatter | solution.py:25
  12.4 0.8 copy.22
  13.2 0.2 reshape.75
  13.4 3.9 %gather_fusion = bf16[576]{0:T(1024)(128)(2,1)S(1)} fusion(bf16[384]{0:T(512)(128)(2,1)S(1)} %reshape.75, s32[1024]{0:T(1024)S(1)} %pad_clamp_fusion.2), kind=kCustom, calls=%fused_computation | custom fusion | bytes 4608 | tf_op jit(solution)/shard_map/gather | solution.py:33
  17.3 0.7 all_to_all.20
  18.0 6.3 %all-to-all-start = ((bf16[8,1,72]{2,1,0:T(2,128)(2,1)}), bf16[8,1,72]{2,1,0:T(2,128)(2,1)S(1)}, u32[]{:S(2)}, u32[]{:S(2)}) async-start(bf16[8,1,72]{2,1,0:T(2,128)(2,1)} %all_to_all.20), calls=%async_computation | async-start | bytes 8192 | tf_op jit(solution)/shard_map/all_to_all | solution.py:43
  24.4 0.7 all-gather.3.cloned.1.call-update
  25.2 3.4 %gather_fusion.1 = bf16[576,2048]{1,0:T(8,128)(2,1)S(1)} fusion(bf16[192,2048]{1,0:T(8,128)(2,1)S(1)} %copy-done, s32[1024]{0:T(1024)S(1)} %pad_clamp_fusion.1), kind=kCustom, calls=%fused_computation.1 | custom fusion | bytes 4720896 | tf_op jit(solution)/shard_map/gather | solution.py:30
  28.6 1.7 %broadcast_select_fusion = bf16[8,72,2048]{2,1,0:T(8,128)(2,1)} fusion(bf16[8,72,2048]{2,1,0:T(8,128)(2,1)S(1)} %bitcast.15, pred[8,72]{1,0:T(8,128)(4,1)S(1)} %broadcast_in_dim.44), kind=kLoop, calls=%fused_computation.10 | loop fusion | flops 1179648 | bytes 4719168 | tf_op jit(solution)/shard_map/jit(_where)/select_n | solution.py:29
  30.3 5.1 %all-to-all-start.1 = ((bf16[8,72,2048]{2,1,0:T(8,128)(2,1)}), bf16[8,72,2048]{2,1,0:T(8,128)(2,1)S(1)}, u32[]{:S(2)}, u32[]{:S(2)}) async-start(bf16[8,72,2048]{2,1,0:T(8,128)(2,1)} %broadcast_select_fusion), calls=%async_computation.1 | async-start | bytes 4718592 | tf_op jit(solution)/shard_map/all_to_all | solution.py:36
  35.5 54.5 %all-to-all-done.1 = bf16[8,72,2048]{2,1,0:T(8,128)(2,1)S(1)} async-done(((bf16[8,72,2048]{2,1,0:T(8,128)(2,1)}), bf16[8,72,2048]{2,1,0:T(8,128)(2,1)S(1)}, u32[]{:S(2)}, u32[]{:S(2)}) %all-to-all-start.1) | async-done | bytes 2359328 | tf_op jit(solution)/shard_map/all_to_all | solution.py:36
  90.1 5.5 %fusion.2 = bf16[768,2048]{0,1:T(8,128)(2,1)} fusion(bf16[576,768]{1,0:T(8,128)(2,1)} %param.8, bf16[576,2048]{1,0:T(8,128)(2,1)S(1)} %bitcast.16, f32[576]{0:T(1024)S(1)} %reshape.79), kind=kOutput, calls=%fused_computation.8 | convolution fusion | flops 1817051136 | bytes 6392064 | tf_op jit(solution)/shard_map/dot_general | solution.py:61
  95.6 4.7 %copy.26 = bf16[768,2048]{1,0:T(8,128)(2,1)} copy(bf16[768,2048]{0,1:T(8,128)(2,1)} %fusion.2) | data formatting | bytes 6291456
  100.3 5.1 %multiply_reduce_fusion = (f32[576]{0:T(1024)S(1)}, bf16[576,768]{1,0:T(8,128)(2,1)}) fusion(bf16[576,768]{1,0:T(8,128)(2,1)} %param.8, f32[576]{0:T(1024)S(1)} %reshape.79, bf16[576,2048]{1,0:T(8,128)(2,1)S(1)} %bitcast.17, bf16[1,768,2048]{2,1,0:T(8,128)(2,1)} %all-gather.3.cloned.1.call-done), kind=kOutput, calls=%fused_computation.11 | convolution fusion | flops 1814150656 | bytes 7279104 | tf_op jit(solution)/shard_map/dot_general | solution.py:57
  105.4 0.7 all_to_all.18
  106.1 3.3 %all-to-all-start.2 = ((f32[8,1,72]{2,1,0:T(1,128)}), f32[8,1,72]{2,1,0:T(1,128)S(1)}, u32[]{:S(2)}, u32[]{:S(2)}) async-start(f32[8,1,72]{2,1,0:T(1,128)} %all_to_all.18), calls=%async_computation.2 | async-start | bytes 8192 | tf_op jit(solution)/shard_map/all_to_all | solution.py:68
  109.4 5.4 %all-to-all-done.2 = f32[8,1,72]{2,1,0:T(1,128)S(1)} async-done(((f32[8,1,72]{2,1,0:T(1,128)}), f32[8,1,72]{2,1,0:T(1,128)S(1)}, u32[]{:S(2)}, u32[]{:S(2)}) %all-to-all-start.2) | async-done | bytes 2336 | tf_op jit(solution)/shard_map/all_to_all | solution.py:68
  114.8 0.5 broadcast.69
  115.3 0.7 reduce.9
  116.1 1.9 %gather_fusion.2 = f32[384]{0:T(512)S(1)} fusion(f32[576]{0:T(1024)S(1)} %reshape.77, s32[1024]{0:T(1024)S(1)} %pad_clamp_fusion), kind=kCustom, calls=%fused_computation.2 | custom fusion | bytes 4608 | tf_op jit(solution)/shard_map/gather | solution.py:71
  118.0 0.1 reshape.78
  118.1 0.7 copy.25
  118.8 24.6 %reduce-scatter.4.cloned.1.call-done = bf16[192,2048]{1,0:T(8,128)(2,1)} async-done(((bf16[768,2048]{1,0:T(8,128)(2,1)}), bf16[192,2048]{1,0:T(8,128)(2,1)}) %reduce-scatter.4.cloned.1.call-update) | async-done | bytes 786448
  143.3 2.2 %copy.27 = bf16[192,2048]{0,1:T(8,128)(2,1)} copy(bf16[192,2048]{1,0:T(8,128)(2,1)} %reduce-scatter.4.cloned.1.call-done) | data formatting | bytes 1572864
  145.6 1.4 bitcast_convert_fusion
  146.9 1.7 %copy.24 = f32[1,192,2048]{2,1,0:T(8,128)} copy(f32[1,192,2048]{1,2,0:T(8,128)S(1)} %bitcast_convert_fusion) | data formatting | bytes 3145728
  (19 shorter events, 0.4 us)
Async XLA Ops:
  7.2 18.0 %copy-start = (bf16[192,2048]{1,0:T(8,128)(2,1)S(1)}, bf16[192,2048]{1,0:T(8,128)(2,1)}, u32[]{:S(2)}) copy-start(bf16[192,2048]{1,0:T(8,128)(2,1)} %param.5) | copy-start | bytes 2359300
  18.0 12.3 %all-to-all-start = ((bf16[8,1,72]{2,1,0:T(2,128)(2,1)}), bf16[8,1,72]{2,1,0:T(2,128)(2,1)S(1)}, u32[]{:S(2)}, u32[]{:S(2)}) async-start(bf16[8,1,72]{2,1,0:T(2,128)(2,1)} %all_to_all.20), calls=%async_computation | async-start | bytes 8192 | tf_op jit(solution)/shard_map/all_to_all | solution.py:43
  24.3 76.0 %all-gather.3.cloned.1.call-start = ((), (), s32[]{:S(2)}) async-start(), calls=%async_computation.4 | async-start | bytes 3932160 | tf_op jit(solution)/shard_map/all_gather | solution.py:56
  30.3 59.8 %all-to-all-start.1 = ((bf16[8,72,2048]{2,1,0:T(8,128)(2,1)}), bf16[8,72,2048]{2,1,0:T(8,128)(2,1)S(1)}, u32[]{:S(2)}, u32[]{:S(2)}) async-start(bf16[8,72,2048]{2,1,0:T(8,128)(2,1)} %broadcast_select_fusion), calls=%async_computation.1 | async-start | bytes 4718592 | tf_op jit(solution)/shard_map/all_to_all | solution.py:36
  35.4 108.0 %reduce-scatter.4.cloned.1.call-start = ((), (), s32[]{:S(2)}) async-start(), calls=%async_computation.5 | async-start | bytes 3932160
  106.1 8.7 %all-to-all-start.2 = ((f32[8,1,72]{2,1,0:T(1,128)}), f32[8,1,72]{2,1,0:T(1,128)S(1)}, u32[]{:S(2)}, u32[]{:S(2)}) async-start(f32[8,1,72]{2,1,0:T(1,128)} %all_to_all.18), calls=%async_computation.2 | async-start | bytes 8192 | tf_op jit(solution)/shard_map/all_to_all | solution.py:68
Sparse Core Ops, SparseCore 0:
  27.0 45.4 all-gather.2
  100.4 42.8 reduce-scatter.3
where the time goes:
time: 156 us; the launch traced here: 155 us
  waiting for transfers between devices  85.2 us (55%)
  local copies, waits for them, and re-layouts  25.9 us (17%)
  starting transfers between devices  14.8 us (9%)
  between operations  14.2 us (9%)
  matrix products  10.6 us (7%)
  other arithmetic  4.73 us (3%)
    all_to_all x1, waiting for transfers between devices, per_device(): lax.all_to_all(send_rows.reshape(experts, capacity, features), 'expert',...  54.5 us
    unnamed x3, waiting for transfers between devices  25.3 us
    unnamed x8, local copies, waits for them, and re-layouts  11 us
    all_to_all x1, starting transfers between devices, per_device(): lax.all_to_all(send_weights.reshape(experts, capacity), 'expert', split_a...  6.33 us
    dot_general x1, matrix products, per_device(): lax.dot_general(saved_hidden, weighted, (((0,), (0,)), ((), ())), preferr...  5.51 us
    all_to_all x1, waiting for transfers between devices, per_device(): lax.all_to_all(route_terms.reshape(experts, capacity), 'expert', split_ax...  5.4 us
    all_to_all x1, starting transfers between devices, per_device(): lax.all_to_all(send_rows.reshape(experts, capacity, features), 'expert',...  5.09 us
    dot_general x1, matrix products, per_device(): lax.dot_general(grad_rows, full_weight, contract, preferred_element_type=...  5.08 us
  transfers between devices with their start and end apart: 5, of which 3 were waited for; matrix products, arithmetic and copies ran while one was open for 16% of the time, Pallas kernels for 0%

commit v1 on v0

--- a/solution.py
+++ b/solution.py
@@ -1,7 +1,39 @@
+import functools
 import jax
 import jax.numpy as jnp
 from jax import lax
 from jax.sharding import PartitionSpec as P
+
+
+def write_frames(sample, d_out, panel):
+    fresh = sample.shape
+    return jnp.moveaxis(
+        sample.reshape(*fresh[:d_out], panel, fresh[d_out] // panel, *fresh[d_out + 1 :]), d_out, 0
+    )
+
+
+def see_plate_on_mesh(sheet, ndim_at):
+    sheet = jnp.moveaxis(sheet, 0, ndim_at)
+    outcome_arr = sheet.shape
+    return sheet.reshape(
+        *outcome_arr[:ndim_at],
+        outcome_arr[ndim_at] * outcome_arr[ndim_at + 1],
+        *outcome_arr[ndim_at + 2 :]
+    )
+
+
+def form_column(x_local, axis_tag, obj, s0):
+    part_next, u_next = (lax.axis_size(axis_tag), lax.axis_index(axis_tag))
+    moved = write_frames(x_local, obj, part_next)
+    panels = [moved[u_next]]
+    for rr in [*range(1, part_next)]:
+        u1 = moved[u_next ^ rr]
+        panels.append(lax.ppermute(u1, axis_tag, [(jj, jj ^ rr) for jj in range(part_next)]))
+    moved = jnp.stack(panels)[u_next ^ jnp.arange(part_next)]
+    return see_plate_on_mesh(moved, s0)
+
+
+clear_trees_by_axis = functools.partial(form_column, axis_tag="expert", obj=0, s0=0)
 
 
 def route_slots(routes, experts, capacity):
@@ -40,13 +72,7 @@
             concat_axis=0,
             tiled=True,
         ),
-        lax.all_to_all(
-            send_weights.reshape(experts, capacity),
-            "expert",
-            split_axis=0,
-            concat_axis=0,
-            tiled=True,
-        ),
+        clear_trees_by_axis(send_weights.reshape(experts, capacity)),
     )
     grad_rows = recv_rows.reshape(slot_count, features)
     slot_weights = recv_weights.reshape(slot_count).astype(jnp.float32)

time: 156 us -> 146 us (0.936)
  waiting for transfers between devices: 85.2 us -> 69.8 us
  starting transfers between devices: 14.8 us -> 21 us
    all_to_all x1, waiting for transfers between devices: 54.5 us -> 0.01 us  [per_device(): lax.all_to_all(send_rows.reshape(experts, capacity, features), 'expert',...]
    ppermute x0 -> x7, waiting for transfers between devices: none -> 39.2 us  [form_column(): lax.ppermute(u1, axis_tag, [(jj, jj ^ rr) for jj in range(part_next)])]
    ppermute x0 -> x7, starting transfers between devices: none -> 11.1 us  [form_column(): lax.ppermute(u1, axis_tag, [(jj, jj ^ rr) for jj in range(part_next)])]
    all_to_all x1 -> x0, starting transfers between devices: 6.33 us -> none  [per_device(): lax.all_to_all(send_weights.reshape(experts, capacity), 'expert', split_a...]
    unnamed x8 -> x10, local copies, waits for them, and re-layouts: 11 us -> 10.2 us
  transfers between devices with their start and end apart: 5 -> 11, of which waited for: 3 -> 4; matrix products, arithmetic and copies ran while one was open for 16% -> 24% of each run, Pallas kernels for 0% -> 0%
where the time goes in v1:
time: 146 us
  waiting for transfers between devices  69.8 us (48%)
  local copies, waits for them, and re-layouts  25.2 us (17%)
  starting transfers between devices  21 us (14%)
  between operations  14.3 us (10%)
  matrix products  10.6 us (7%)
  other arithmetic  4.74 us (3%)
    ppermute x7, waiting for transfers between devices, form_column(): lax.ppermute(u1, axis_tag, [(jj, jj ^ rr) for jj in range(part_next)])  39.2 us
    unnamed x3, waiting for transfers between devices  25.2 us
    ppermute x7, starting transfers between devices, form_column(): lax.ppermute(u1, axis_tag, [(jj, jj ^ rr) for jj in range(part_next)])  11.1 us
    unnamed x10, local copies, waits for them, and re-layouts  10.2 us
    all_to_all x1, starting transfers between devices, per_device(): lax.all_to_all(send_rows.reshape(experts, capacity, features), 'expert',...  6.46 us
    dot_general x1, matrix products, per_device(): lax.dot_general(saved_hidden, weighted, (((0,), (0,)), ((), ())), preferr...  5.52 us
    all_to_all x1, waiting for transfers between devices, per_device(): lax.all_to_all(route_terms.reshape(experts, capacity), 'expert', split_ax...  5.4 us
    dot_general x1, matrix products, per_device(): lax.dot_general(grad_rows, full_weight, contract, preferred_element_type=...  5.09 us
  transfers between devices with their start and end apart: 11, of which 4 were waited for; matrix products, arithmetic and copies ran while one was open for 24% of the time, Pallas kernels for 0%

profile of v1, /device:TPU:0, one launch (start us, length us, event | category | flops | bytes accessed | tf_op | source)
XLA Modules:
  0.0 145.7 jit_solution(3560568505112745782)
XLA Ops:
  7.2 0.7 all-gather.3.cloned.1.call-update
  7.9 0.7 broadcast_multiply_fusion
  8.6 0.8 copy.41
  9.8 0.2 convert_reduce_fusion
  10.1 2.9 %scatter_custom_fusion = s32[576]{0:T(1024)S(1)} fusion(s32[384]{0:T(512)S(1)} %fusion.9, s32[384]{0:T(512)S(1)} %iota.14, s32[]{:T(128)} %constant.17.clone.1), kind=kCustom, calls=%fused_computation.42 | custom fusion | bytes 2308 | tf_op jit(solution)/shard_map/scatter | solution.py:57
  13.2 3.4 %gather_fusion.2 = bf16[576,2048]{1,0:T(8,128)(2,1)S(1)} fusion(bf16[192,2048]{1,0:T(8,128)(2,1)S(1)} %copy-done, s32[1024]{0:T(1024)S(1)} %pad_clamp_fusion.1), kind=kCustom, calls=%fused_computation.2 | custom fusion | bytes 4720896 | tf_op jit(solution)/shard_map/gather | solution.py:62
  16.6 1.7 %broadcast_select_fusion = bf16[8,72,2048]{2,1,0:T(8,128)(2,1)} fusion(bf16[8,72,2048]{2,1,0:T(8,128)(2,1)S(1)} %bitcast.53, pred[8,72]{1,0:T(8,128)(4,1)S(1)} %broadcast_in_dim.45), kind=kLoop, calls=%fused_computation.11 | loop fusion | flops 1179648 | bytes 4719168 | tf_op jit(solution)/shard_map/jit(_where)/select_n | solution.py:61
  18.3 6.5 %all-to-all-start = ((bf16[8,72,2048]{2,1,0:T(8,128)(2,1)}), bf16[8,72,2048]{2,1,0:T(8,128)(2,1)S(1)}, u32[]{:S(2)}, u32[]{:S(2)}) async-start(bf16[8,72,2048]{2,1,0:T(8,128)(2,1)} %broadcast_select_fusion), calls=%async_computation | async-start | bytes 4718592 | tf_op jit(solution)/shard_map/all_to_all | solution.py:68
  25.0 0.2 reshape.85
  25.1 3.9 %gather_fusion = bf16[576]{0:T(1024)(128)(2,1)S(1)} fusion(bf16[384]{0:T(512)(128)(2,1)S(1)} %reshape.85, s32[1024]{0:T(1024)S(1)} %pad_clamp_fusion.3), kind=kCustom, calls=%fused_computation | custom fusion | bytes 4608 | tf_op jit(solution)/shard_map/gather | solution.py:65
  29.2 0.5 collective-permute-start
  29.7 1.7 %collective-permute-start.1 = (bf16[1,72]{1,0:T(2,128)(2,1)S(1)}, bf16[1,72]{1,0:T(2,128)(2,1)S(1)}, u32[]{:S(2)}, u32[]{:S(2)}) collective-permute-start(bf16[1,72]{1,0:T(2,128)(2,1)S(1)} %get-tuple-element.24), channel_id=1, source_target_pairs={{0,2},{1,3},{2,0},{3,1},{4,6},{5,7},{6,4},{7,5},{8,10},{9,11},{10,... | collective-permute-start | bytes 440 | tf_op jit(solution)/shard_map/ppermute | solution.py:31
  31.4 2.6 %collective-permute-start.3 = (bf16[1,72]{1,0:T(2,128)(2,1)S(1)}, bf16[1,72]{1,0:T(2,128)(2,1)S(1)}, u32[]{:S(2)}, u32[]{:S(2)}) collective-permute-start(bf16[1,72]{1,0:T(2,128)(2,1)S(1)} %get-tuple-element.22), channel_id=1, source_target_pairs={{0,4},{1,5},{2,6},{3,7},{4,0},{5,1},{6,2},{7,3},{8,12},{9,13},{10,... | collective-permute-start | bytes 440 | tf_op jit(solution)/shard_map/ppermute | solution.py:31
  34.1 3.5 %collective-permute-start.5 = (bf16[1,72]{1,0:T(2,128)(2,1)S(1)}, bf16[1,72]{1,0:T(2,128)(2,1)S(1)}, u32[]{:S(2)}, u32[]{:S(2)}) collective-permute-start(bf16[1,72]{1,0:T(2,128)(2,1)S(1)} %get-tuple-element.20), channel_id=1, source_target_pairs={{0,6},{1,7},{2,4},{3,5},{4,2},{5,3},{6,0},{7,1},{8,14},{9,15},{10,... | collective-permute-start | bytes 440 | tf_op jit(solution)/shard_map/ppermute | solution.py:31
  37.7 26.3 %collective-permute-done.1 = bf16[1,72]{1,0:T(2,128)(2,1)S(1)} collective-permute-done((bf16[1,72]{1,0:T(2,128)(2,1)S(1)}, bf16[1,72]{1,0:T(2,128)(2,1)S(1)}, u32[]{:S(2)}, u32[]{:S(2)}) %collective-permute-start.1) | collective-permute-done | bytes 176 | tf_op jit(solution)/shard_map/ppermute | solution.py:31
  63.9 2.7 %collective-permute-start.6 = (bf16[1,72]{1,0:T(2,128)(2,1)S(1)}, bf16[1,72]{1,0:T(2,128)(2,1)S(1)}, u32[]{:S(2)}, u32[]{:S(2)}) collective-permute-start(bf16[1,72]{1,0:T(2,128)(2,1)S(1)} %get-tuple-element.19), channel_id=1, source_target_pairs={{0,7},{1,6},{2,5},{3,4},{4,3},{5,2},{6,1},{7,0},{8,15},{9,14},{10,... | collective-permute-start | bytes 440 | tf_op jit(solution)/shard_map/ppermute | solution.py:31
  66.6 12.9 %collective-permute-done.3 = bf16[1,72]{1,0:T(2,128)(2,1)S(1)} collective-permute-done((bf16[1,72]{1,0:T(2,128)(2,1)S(1)}, bf16[1,72]{1,0:T(2,128)(2,1)S(1)}, u32[]{:S(2)}, u32[]{:S(2)}) %collective-permute-start.3) | collective-permute-done | bytes 176 | tf_op jit(solution)/shard_map/ppermute | solution.py:31
  79.6 0.6 gather_fusion.1
  80.2 5.5 %fusion.2 = bf16[768,2048]{0,1:T(8,128)(2,1)} fusion(bf16[576,768]{1,0:T(8,128)(2,1)} %param.8, bf16[576,2048]{1,0:T(8,128)(2,1)S(1)} %bitcast.54, f32[576]{0:T(1024)S(1)} %reshape.89), kind=kOutput, calls=%fused_computation.9 | convolution fusion | flops 1817051136 | bytes 6392064 | tf_op jit(solution)/shard_map/dot_general | solution.py:87
  85.8 4.7 %copy.52 = bf16[768,2048]{1,0:T(8,128)(2,1)} copy(bf16[768,2048]{0,1:T(8,128)(2,1)} %fusion.2) | data formatting | bytes 6291456
  90.5 5.1 %multiply_reduce_fusion = (f32[576]{0:T(1024)S(1)}, bf16[576,768]{1,0:T(8,128)(2,1)}) fusion(bf16[576,768]{1,0:T(8,128)(2,1)} %param.8, f32[576]{0:T(1024)S(1)} %reshape.89, bf16[576,2048]{1,0:T(8,128)(2,1)S(1)} %bitcast.55, bf16[1,768,2048]{2,1,0:T(8,128)(2,1)} %all-gather.3.cloned.1.call-done), kind=kOutput, calls=%fused_computation.12 | convolution fusion | flops 1814150656 | bytes 7279104 | tf_op jit(solution)/shard_map/dot_general | solution.py:83
  95.6 0.7 all_to_all.10
  96.3 3.3 %all-to-all-start.1 = ((f32[8,1,72]{2,1,0:T(1,128)}), f32[8,1,72]{2,1,0:T(1,128)S(1)}, u32[]{:S(2)}, u32[]{:S(2)}) async-start(f32[8,1,72]{2,1,0:T(1,128)} %all_to_all.10), calls=%async_computation.1 | async-start | bytes 8192 | tf_op jit(solution)/shard_map/all_to_all | solution.py:94
  99.6 5.4 %all-to-all-done.1 = f32[8,1,72]{2,1,0:T(1,128)S(1)} async-done(((f32[8,1,72]{2,1,0:T(1,128)}), f32[8,1,72]{2,1,0:T(1,128)S(1)}, u32[]{:S(2)}, u32[]{:S(2)}) %all-to-all-start.1) | async-done | bytes 2336 | tf_op jit(solution)/shard_map/all_to_all | solution.py:94
  105.0 0.5 broadcast.105
  105.5 0.7 reduce.5
  106.3 1.9 %gather_fusion.3 = f32[384]{0:T(512)S(1)} fusion(f32[576]{0:T(1024)S(1)} %reshape.87, s32[1024]{0:T(1024)S(1)} %pad_clamp_fusion), kind=kCustom, calls=%fused_computation.3 | custom fusion | bytes 4608 | tf_op jit(solution)/shard_map/gather | solution.py:97
  108.3 0.7 copy.51
  109.0 24.5 %reduce-scatter.4.cloned.1.call-done = bf16[192,2048]{1,0:T(8,128)(2,1)} async-done(((bf16[768,2048]{1,0:T(8,128)(2,1)}), bf16[192,2048]{1,0:T(8,128)(2,1)}) %reduce-scatter.4.cloned.1.call-update) | async-done | bytes 786448
  133.5 2.2 %copy.53 = bf16[192,2048]{0,1:T(8,128)(2,1)} copy(bf16[192,2048]{1,0:T(8,128)(2,1)} %reduce-scatter.4.cloned.1.call-done) | data formatting | bytes 1572864
  135.7 1.4 bitcast_convert_fusion
  137.1 1.7 %copy.50 = f32[1,192,2048]{2,1,0:T(8,128)} copy(f32[1,192,2048]{1,2,0:T(8,128)S(1)} %bitcast_convert_fusion) | data formatting | bytes 3145728
  (37 shorter events, 1.4 us)
Async XLA Ops:
  7.2 6.0 %copy-start = (bf16[192,2048]{1,0:T(8,128)(2,1)S(1)}, bf16[192,2048]{1,0:T(8,128)(2,1)}, u32[]{:S(2)}) copy-start(bf16[192,2048]{1,0:T(8,128)(2,1)} %param.5) | copy-start | bytes 2359300
  7.2 83.3 %all-gather.3.cloned.1.call-start = ((), (), s32[]{:S(2)}) async-start(), calls=%async_computation.3 | async-start | bytes 3932160 | tf_op jit(solution)/shard_map/all_gather | solution.py:82
  18.3 6.5 %copy-start.1 = (bf16[192,2]{0,1:T(2,128)(2,1)S(1)}, bf16[192,2]{0,1:T(2,128)(2,1)}, u32[]{:S(2)}) copy-start(bf16[192,2]{0,1:T(2,128)(2,1)} %param.7) | copy-start | bytes 2308
  18.3 62.0 %all-to-all-start = ((bf16[8,72,2048]{2,1,0:T(8,128)(2,1)}), bf16[8,72,2048]{2,1,0:T(8,128)(2,1)S(1)}, u32[]{:S(2)}, u32[]{:S(2)}) async-start(bf16[8,72,2048]{2,1,0:T(8,128)(2,1)} %broadcast_select_fusion), calls=%async_computation | async-start | bytes 4718592 | tf_op jit(solution)/shard_map/all_to_all | solution.py:68
  24.7 108.8 %reduce-scatter.4.cloned.1.call-start = ((), (), s32[]{:S(2)}) async-start(), calls=%async_computation.4 | async-start | bytes 3932160
  29.2 4.9 %collective-permute-start = (bf16[1,72]{1,0:T(2,128)(2,1)S(1)}, bf16[1,72]{1,0:T(2,128)(2,1)S(1)}, u32[]{:S(2)}, u32[]{:S(2)}) collective-permute-start(bf16[1,72]{1,0:T(2,128)(2,1)S(1)} %get-tuple-element.25), channel_id=1, source_target_pairs={{0,1},{1,0},{2,3},{3,2},{4,5},{5,4},{6,7},{7,6},{8,9},{9,8},{10,11... | collective-permute-start | bytes 440 | tf_op jit(solution)/shard_map/ppermute | solution.py:31
  29.7 34.2 %collective-permute-start.1 = (bf16[1,72]{1,0:T(2,128)(2,1)S(1)}, bf16[1,72]{1,0:T(2,128)(2,1)S(1)}, u32[]{:S(2)}, u32[]{:S(2)}) collective-permute-start(bf16[1,72]{1,0:T(2,128)(2,1)S(1)} %get-tuple-element.24), channel_id=1, source_target_pairs={{0,2},{1,3},{2,0},{3,1},{4,6},{5,7},{6,4},{7,5},{8,10},{9,11},{10,... | collective-permute-start | bytes 440 | tf_op jit(solution)/shard_map/ppermute | solution.py:31
  31.4 35.2 %collective-permute-start.2 = (bf16[1,72]{1,0:T(2,128)(2,1)S(1)}, bf16[1,72]{1,0:T(2,128)(2,1)S(1)}, u32[]{:S(2)}, u32[]{:S(2)}) collective-permute-start(bf16[1,72]{1,0:T(2,128)(2,1)S(1)} %get-tuple-element.23), channel_id=1, source_target_pairs={{0,3},{1,2},{2,1},{3,0},{4,7},{5,6},{6,5},{7,4},{8,11},{9,10},{10,... | collective-permute-start | bytes 440 | tf_op jit(solution)/shard_map/ppermute | solution.py:31
  31.4 48.1 %collective-permute-start.3 = (bf16[1,72]{1,0:T(2,128)(2,1)S(1)}, bf16[1,72]{1,0:T(2,128)(2,1)S(1)}, u32[]{:S(2)}, u32[]{:S(2)}) collective-permute-start(bf16[1,72]{1,0:T(2,128)(2,1)S(1)} %get-tuple-element.22), channel_id=1, source_target_pairs={{0,4},{1,5},{2,6},{3,7},{4,0},{5,1},{6,2},{7,3},{8,12},{9,13},{10,... | collective-permute-start | bytes 440 | tf_op jit(solution)/shard_map/ppermute | solution.py:31
  34.0 45.6 %collective-permute-start.4 = (bf16[1,72]{1,0:T(2,128)(2,1)S(1)}, bf16[1,72]{1,0:T(2,128)(2,1)S(1)}, u32[]{:S(2)}, u32[]{:S(2)}) collective-permute-start(bf16[1,72]{1,0:T(2,128)(2,1)S(1)} %get-tuple-element.21), channel_id=1, source_target_pairs={{0,5},{1,4},{2,7},{3,6},{4,1},{5,0},{6,3},{7,2},{8,13},{9,12},{10,... | collective-permute-start | bytes 440 | tf_op jit(solution)/shard_map/ppermute | solution.py:31
  34.1 45.4 %collective-permute-start.5 = (bf16[1,72]{1,0:T(2,128)(2,1)S(1)}, bf16[1,72]{1,0:T(2,128)(2,1)S(1)}, u32[]{:S(2)}, u32[]{:S(2)}) collective-permute-start(bf16[1,72]{1,0:T(2,128)(2,1)S(1)} %get-tuple-element.20), channel_id=1, source_target_pairs={{0,6},{1,7},{2,4},{3,5},{4,2},{5,3},{6,0},{7,1},{8,14},{9,15},{10,... | collective-permute-start | bytes 440 | tf_op jit(solution)/shard_map/ppermute | solution.py:31
  63.9 15.6 %collective-permute-start.6 = (bf16[1,72]{1,0:T(2,128)(2,1)S(1)}, bf16[1,72]{1,0:T(2,128)(2,1)S(1)}, u32[]{:S(2)}, u32[]{:S(2)}) collective-permute-start(bf16[1,72]{1,0:T(2,128)(2,1)S(1)} %get-tuple-element.19), channel_id=1, source_target_pairs={{0,7},{1,6},{2,5},{3,4},{4,3},{5,2},{6,1},{7,0},{8,15},{9,14},{10,... | collective-permute-start | bytes 440 | tf_op jit(solution)/shard_map/ppermute | solution.py:31
  96.3 8.7 %all-to-all-start.1 = ((f32[8,1,72]{2,1,0:T(1,128)}), f32[8,1,72]{2,1,0:T(1,128)S(1)}, u32[]{:S(2)}, u32[]{:S(2)}) async-start(f32[8,1,72]{2,1,0:T(1,128)} %all_to_all.10), calls=%async_computation.1 | async-start | bytes 8192 | tf_op jit(solution)/shard_map/all_to_all | solution.py:94
Sparse Core Ops, SparseCore 0:
  9.9 46.6 all-gather.2
  90.6 42.8 reduce-scatter.3
